TPU v7x, 32 devices: a whole 2x2x4 slice. The times are simulated.
32 devices in a mesh: member: 8 (over y, x, core), tile: 4 (over z).
Axes of the slice: x: 2, y: 2, z: 4, core: 2. Of those that a mesh axis runs over, the one named last changes fastest.
Arguments:
- state: float32 [8, 3, 4, 384, 512], P('member', None, None, 'tile'), may hold values from -6 to 6
- stiffness: float32 [4, 384, 512], P(None, 'tile'), may hold values from 0.1 to 0.45
- driver: float32 [16, 12, 512], P('tile', None, 'member'), may hold values from -6 to 6
- zone_rows: int32 [16], replicated, may hold values from 0 to 15, as said below
- zone_depth: int32 [8], P('member'), may hold values from 1 to 8, as said below
Outputs:
- advanced: float32 [8, 3, 4, 384, 512], P('member', None, None, 'tile')
Inputs may be any that keep to these rules, and one draw needn't show every extreme that they name: `zone_rows`: the entries are a permutation of the zone rows; driver rows 0 to 7 carry the zone rows 8 to 15, the others the zone rows 0 to 7. `zone_depth`: some member has depth 8.
All inputs are finite; a program needn't handle non-finite values.
Results may differ from a plain program's by a relative error of at most 0.0003.
Values sent between devices are 32-bit elements; how exact they have to be, the bound alone decides.
A program may use at most 64 MiB of HBM per device.

v0:
```python
import jax
import jax.numpy as jnp
from jax import lax
from jax.sharding import PartitionSpec as P

ZONE = 8
SUBSTEPS = 3


relax_peak = 0.9


def from_behind(block, axis, distance):
    devices = range(lax.axis_size(axis))
    route = [(i - distance, i) for i in devices if i - distance in devices]
    return lax.ppermute(block, axis, route)


def with_halo(block, sides, width):
    for axis, dim in sides:
        count = lax.axis_size(axis)
        forward = [(i, i + 1) for i in range(count - 1)]
        backward = [(target, source) for source, target in forward]
        low = lax.ppermute(
            lax.slice_in_dim(block, block.shape[dim] - width, None, axis=dim), axis, forward
        )
        high = lax.ppermute(lax.slice_in_dim(block, 0, width, axis=dim), axis, backward)
        block = jnp.concatenate([low, block, high], axis=dim)
    return block


def shift_down(field):
    return jnp.concatenate([jnp.zeros_like(field[..., :1, :]), field[..., :-1, :]], axis=-2)


def shift_up(field):
    return jnp.concatenate([field[..., 1:, :], jnp.zeros_like(field[..., :1, :])], axis=-2)


def zone_geometry(rows_global, grid_rows, depths, zone_rows, driver_all, levels, columns):
    inside = (rows_global >= 0) & (rows_global < grid_rows)
    top_rows = inside & (rows_global < ZONE)
    bottom_rows = inside & (rows_global >= grid_rows - ZONE)
    distance_int = jnp.where(top_rows, rows_global, grid_rows - 1 - rows_global)
    distance = distance_int.astype(jnp.float32)
    depth_float = depths.astype(jnp.float32)[:, None]
    ratio = (depth_float - distance[None, :]) / depth_float
    in_zone = (top_rows | bottom_rows)[None, :] & (distance[None, :] < depth_float)
    weights = jnp.where(in_zone, relax_peak * ratio * ratio, jnp.float32(0.0))
    zone_index = jnp.where(
        top_rows, rows_global, jnp.where(bottom_rows, ZONE + grid_rows - 1 - rows_global, -1)
    )
    selector = (zone_index[:, None] == zone_rows[None, :]).astype(jnp.float32)
    targets = jnp.einsum("rz,zcy->cry", selector, driver_all, precision=lax.Precision.HIGHEST)
    targets = targets.reshape(3, levels, rows_global.shape[0], columns)
    return (inside[:, None], weights[:, None, None, :, None], targets)


def advance(fields, stiff_rows, inside, weights, targets):
    pressure, along_x, along_y = (fields[:, 0], fields[:, 1], fields[:, 2])
    pressure = pressure - stiff_rows * (
        along_x - shift_down(along_x) + (along_y - jnp.roll(along_y, 1, -1))
    )
    pressure = jnp.where(inside, pressure, jnp.float32(0.0))
    along_x = along_x - (shift_up(pressure) - pressure)
    along_x = jnp.where(inside, along_x, jnp.float32(0.0))
    along_y = along_y - (jnp.roll(pressure, -1, -1) - pressure)
    along_y = jnp.where(inside, along_y, jnp.float32(0.0))
    stacked = jnp.stack([pressure, along_x, along_y], axis=1)
    return stacked + weights * (targets - stacked)


def body(state, stiffness, driver, zone_rows, zone_depth):
    levels = state.shape[2]
    tile_rows = state.shape[3]
    columns = state.shape[4]
    tiles = lax.axis_size("tile")
    grid_rows = tile_rows * tiles
    position = lax.axis_index("tile")
    driver_piece = lax.all_gather(driver, "member", axis=2, tiled=True)
    driver_all = lax.all_gather(driver_piece, "tile", axis=0, tiled=True)
    next_row = from_behind(stiffness[:, :1], "tile", -1)
    stiff_rows = jnp.concatenate([jnp.zeros_like(stiffness[:, :1]), stiffness, next_row], axis=1)
    rows_global = position * tile_rows - 1 + jnp.arange(tile_rows + 2)
    inside, weights, targets = zone_geometry(
        rows_global, grid_rows, zone_depth, zone_rows, driver_all, levels, columns
    )
    fields = state
    for substep in range(SUBSTEPS):
        extended = with_halo(fields, (("tile", 3),), 1)
        extended = advance(extended, stiff_rows, inside, weights, targets)
        fields = extended[:, :, :, 1 : 1 + tile_rows]
    return fields


def solution(mesh):
    in_specs = (
        P("member", None, None, "tile", None),
        P(None, "tile", None),
        P("tile", None, "member"),
        P(),
        P("member"),
    )
    out_specs = P("member", None, None, "tile", None)
    return jax.shard_map(body, mesh=mesh, in_specs=in_specs, out_specs=out_specs, check_vma=False)
```

profile of v0, /device:TPU:0, one launch (start us, length us, event | category | flops | bytes accessed | tf_op | source)
XLA Modules:
  0.0 75.2 jit_solution(3988967024462342036)
XLA Ops:
  0.0 0.0 copy-start.2
  0.0 1.7 %fusion.32 = (f32[1,3,4,1,512]{4,3,2,1,0:T(1,128)}, f32[1,3,4,1,512]{4,3,2,1,0:T(1,128)}) fusion(f32[1,3,4,96,512]{4,3,2,1,0:T(8,128)} %param.5), kind=kLoop, calls=%fused_computation.69 | loop fusion | bytes 98304 | tf_op jit(solution)/shard_map/slice | solution.py:25
  1.7 5.5 %collective-permute-start = (f32[1,3,4,1,512]{4,3,2,1,0:T(1,128)}, f32[1,3,4,1,512]{4,3,2,1,0:T(1,128)}, u32[]{:S(2)}, u32[]{:S(2)}) collective-permute-start(f32[1,3,4,1,512]{4,3,2,1,0:T(1,128)} %get-tuple-element.21), channel_id=1, source_target_pairs={{0,1},{1,2},{2,3},{4,5},{5,6},{6,7},{8,9},{9,10},{10,11},{12,13},{... | collective-permute-start | bytes 73736 | tf_op jit(solution)/shard_map/ppermute | solution.py:24
  7.2 1.3 %collective-permute-start.1 = (f32[1,3,4,1,512]{4,3,2,1,0:T(1,128)}, f32[1,3,4,1,512]{4,3,2,1,0:T(1,128)}, u32[]{:S(2)}, u32[]{:S(2)}) collective-permute-start(f32[1,3,4,1,512]{4,3,2,1,0:T(1,128)} %get-tuple-element.22), channel_id=1, source_target_pairs={{1,0},{2,1},{3,2},{5,4},{6,5},{7,6},{9,8},{10,9},{11,10},{13,12},{... | collective-permute-start | bytes 73736 | tf_op jit(solution)/shard_map/ppermute | solution.py:27
  8.5 1.4 %slice.122 = f32[4,1,512]{2,1,0:T(1,128)} slice(f32[4,96,512]{2,1,0:T(8,128)} %param.6), slice={[0:4], [0:1], [0:512]} | slice | bytes 16384 | tf_op jit(solution)/shard_map/slice | solution.py:82
  9.9 1.3 %collective-permute-start.2 = (f32[4,1,512]{2,1,0:T(1,128)}, f32[4,1,512]{2,1,0:T(1,128)S(1)}, u32[]{:S(2)}, u32[]{:S(2)}) collective-permute-start(f32[4,1,512]{2,1,0:T(1,128)} %slice.122), channel_id=1, source_target_pairs={{1,0},{2,1},{3,2},{5,4},{6,5},{7,6},{9,8},{10,9},{11,10},{13,12},{... | collective-permute-start | bytes 24584 | tf_op jit(solution)/shard_map/ppermute | solution.py:16
  11.2 0.6 select_select_fusion
  11.8 0.9 %copy.6 = f32[4,12,64]{1,0,2:T(4,128)S(1)} copy(f32[4,12,64]{2,0,1:T(4,128)} %param.7) | data formatting | bytes 24576 | tf_op args[2]
  12.7 11.0 %all_gather.6 = f32[4,12,512]{1,0,2:T(4,128)S(1)} all-gather(f32[4,12,64]{1,0,2:T(4,128)S(1)} %copy.6), channel_id=1, replica_groups=mesh['member'=8,'tile'=4] {'member'}, dimensions={2}, use_global_device_ids=true | all-gather | bytes 110592 | tf_op jit(solution)/shard_map/all_gather | solution.py:80
  23.7 0.0 copy-start.1
  23.7 0.4 copy.7
  24.0 18.1 %all_gather.7 = f32[16,12,512]{2,1,0:T(8,128)S(1)} all-gather(f32[4,12,512]{2,1,0:T(8,128)S(1)} %copy.7), channel_id=1, replica_groups=mesh['member'=8,'tile'=4] {'tile'}, dimensions={0}, use_global_device_ids=true | all-gather | bytes 491520 | tf_op jit(solution)/shard_map/all_gather | solution.py:81
  42.8 0.0 copy-done.2
  42.8 2.0 %fusion.23 = f32[98,12,512]{2,0,1:T(8,128)S(1)} fusion(f32[16,12,512]{2,1,0:T(8,128)S(1)} %all_gather.7, s32[98]{0:T(128)} %select_select_fusion, s32[16]{0:T(128)S(1)} %copy-done.2), kind=kOutput, calls=%fused_computation.52 | convolution fusion | flops 115607072 | bytes 2802120 | tf_op jit(solution)/shard_map/rz,zcy->cry/dot_general | solution.py:54
  44.8 0.0 collective-permute-done
  44.8 0.0 collective-permute-done.1
  44.8 0.0 copy-done.1
  44.8 1.1 %pad_maximum_fusion = f32[1,3,4,98,512]{4,3,2,1,0:T(8,128)S(1)} fusion(f32[1,3,4,1,512]{4,3,2,1,0:T(1,128)} %collective-permute-done.1, f32[1,3,4,96,512]{4,3,2,1,0:T(8,128)S(1)} %copy-done.1, f32[1,3,4,1,512]{4,3,2,1,0:T(1,128)} %collective-permute-done), kind=kLoop, calls=%fused_computation | loop fusion | flops 1204224 | bytes 4816896 | tf_op jit(solution)/shard_map/concatenate | solution.py:28
  45.9 0.0 copy-start
  45.9 0.1 slice_bitcast_fusion.7
  46.1 0.1 slice.160
  46.2 0.0 collective-permute-done.2
  46.2 0.8 %copy-done = f32[4,96,512]{2,1,0:T(8,128)S(1)} copy-done((f32[4,96,512]{2,1,0:T(8,128)S(1)}, f32[4,96,512]{2,1,0:T(8,128)}, u32[]{:S(2)}) %copy-start) | copy-done | bytes 786456
  47.0 0.7 fusion.7
  47.8 0.1 slice.162
  47.9 0.3 slice.163
  48.2 0.6 select_bitcast_fusion.2
  48.8 0.8 %multiply_add_fusion.1 = f32[1,3,4,98,512]{4,3,2,1,0:T(8,128)S(1)} fusion(f32[1,3,4,98,512]{4,3,2,1,0:T(8,128)S(1)} %bitcast.91, f32[1,1,4,98,512]{4,3,2,1,0:T(8,128)S(1)} %get-tuple-element.10, f32[1,1,4,98,512]{4,3,2,1,0:T(8,128)S(1)} %get-tuple-element.9, f32[1,1,4,98,512]{4,3,2,1,0:T(8,128)S(1)} %bitcast.95, f32[98]{0:T(128)S(1)} %and_select_fusion), kind=kLoop, calls=%fused_computation.6 | loop fusion | flops 3010560 | bytes 7225736 | tf_op jit(solution)/shard_map/add | solution.py:70
  49.6 3.4 %collective-permute-start.3 = (f32[1,3,4,1,512]{4,3,2,1,0:T(1,128)S(1)}, f32[1,3,4,1,512]{4,3,2,1,0:T(1,128)S(1)}, u32[]{:S(2)}, u32[]{:S(2)}) collective-permute-start(f32[1,3,4,1,512]{4,3,2,1,0:T(1,128)S(1)} %get-tuple-element.17), channel_id=1, source_target_pairs={{0,1},{1,2},{2,3},{4,5},{5,6},{6,7},{8,9},{9,10},{10,11},{12,13},{... | collective-permute-start | bytes 73736 | tf_op jit(solution)/shard_map/ppermute | solution.py:24
  53.1 1.3 %collective-permute-start.4 = (f32[1,3,4,1,512]{4,3,2,1,0:T(1,128)S(1)}, f32[1,3,4,1,512]{4,3,2,1,0:T(1,128)S(1)}, u32[]{:S(2)}, u32[]{:S(2)}) collective-permute-start(f32[1,3,4,1,512]{4,3,2,1,0:T(1,128)S(1)} %get-tuple-element.18), channel_id=1, source_target_pairs={{1,0},{2,1},{3,2},{5,4},{6,5},{7,6},{9,8},{10,9},{11,10},{13,12},{... | collective-permute-start | bytes 73736 | tf_op jit(solution)/shard_map/ppermute | solution.py:27
  54.4 0.3 slice.166
  54.7 0.0 collective-permute-done.3
  54.7 4.1 %collective-permute-done.4 = f32[1,3,4,1,512]{4,3,2,1,0:T(1,128)S(1)} collective-permute-done((f32[1,3,4,1,512]{4,3,2,1,0:T(1,128)S(1)}, f32[1,3,4,1,512]{4,3,2,1,0:T(1,128)S(1)}, u32[]{:S(2)}, u32[]{:S(2)}) %collective-permute-start.4) | collective-permute-done | bytes 24608 | tf_op jit(solution)/shard_map/ppermute | solution.py:27
  58.8 0.3 pad_maximum_fusion.2
  59.1 0.1 slice_bitcast_fusion.4
  59.3 0.1 slice.172
  59.4 0.7 fusion.5
  60.1 0.1 slice.174
  60.2 0.3 slice.175
  60.6 0.5 select_bitcast_fusion.1
  61.1 0.8 %multiply_add_fusion = f32[1,3,4,98,512]{4,3,2,1,0:T(8,128)S(1)} fusion(f32[1,3,4,98,512]{4,3,2,1,0:T(8,128)S(1)} %bitcast.92, f32[1,1,4,98,512]{4,3,2,1,0:T(8,128)S(1)} %get-tuple-element.8, f32[1,1,4,98,512]{4,3,2,1,0:T(8,128)S(1)} %get-tuple-element.7, f32[1,1,4,98,512]{4,3,2,1,0:T(8,128)S(1)} %bitcast.96, f32[98]{0:T(128)S(1)} %and_select_fusion), kind=kLoop, calls=%fused_computation.5 | loop fusion | flops 3010560 | bytes 7225736 | tf_op jit(solution)/shard_map/add | solution.py:70
  62.0 3.0 %collective-permute-start.5 = (f32[1,3,4,1,512]{4,3,2,1,0:T(1,128)S(1)}, f32[1,3,4,1,512]{4,3,2,1,0:T(1,128)S(1)}, u32[]{:S(2)}, u32[]{:S(2)}) collective-permute-start(f32[1,3,4,1,512]{4,3,2,1,0:T(1,128)S(1)} %get-tuple-element.13), channel_id=1, source_target_pairs={{0,1},{1,2},{2,3},{4,5},{5,6},{6,7},{8,9},{9,10},{10,11},{12,13},{... | collective-permute-start | bytes 73736 | tf_op jit(solution)/shard_map/ppermute | solution.py:24
  65.0 1.5 %collective-permute-start.6 = (f32[1,3,4,1,512]{4,3,2,1,0:T(1,128)S(1)}, f32[1,3,4,1,512]{4,3,2,1,0:T(1,128)S(1)}, u32[]{:S(2)}, u32[]{:S(2)}) collective-permute-start(f32[1,3,4,1,512]{4,3,2,1,0:T(1,128)S(1)} %get-tuple-element.14), channel_id=1, source_target_pairs={{1,0},{2,1},{3,2},{5,4},{6,5},{7,6},{9,8},{10,9},{11,10},{13,12},{... | collective-permute-start | bytes 73736 | tf_op jit(solution)/shard_map/ppermute | solution.py:27
  66.5 0.1 slice.190
  66.5 0.3 slice.178
  66.8 0.0 collective-permute-done.5
  66.9 3.8 %collective-permute-done.6 = f32[1,3,4,1,512]{4,3,2,1,0:T(1,128)S(1)} collective-permute-done((f32[1,3,4,1,512]{4,3,2,1,0:T(1,128)S(1)}, f32[1,3,4,1,512]{4,3,2,1,0:T(1,128)S(1)}, u32[]{:S(2)}, u32[]{:S(2)}) %collective-permute-start.6) | collective-permute-done | bytes 24608 | tf_op jit(solution)/shard_map/ppermute | solution.py:27
  70.7 0.4 pad_maximum_fusion.4
  71.1 0.2 slice_bitcast_fusion.1
  71.3 0.1 slice.184
  71.4 0.7 fusion.3
  72.1 0.1 slice.186
  72.2 0.3 slice.187
  72.5 0.5 select_bitcast_fusion
  73.1 2.1 %fusion.1 = f32[1,3,4,96,512]{4,3,2,1,0:T(8,128)} fusion(f32[1,3,4,98,512]{4,3,2,1,0:T(8,128)S(1)} %bitcast.93, f32[1,1,4,98,512]{4,3,2,1,0:T(8,128)S(1)} %get-tuple-element.6, f32[1,1,4,98,512]{4,3,2,1,0:T(8,128)S(1)} %get-tuple-element.5, f32[1,1,4,98,512]{4,3,2,1,0:T(8,128)S(1)} %bitcast.94, f32[96]{0:T(128)S(1)} %slice.190), kind=kLoop, calls=%fused_computation.9 | loop fusion | flops 2949120 | bytes 7127424 | tf_op jit(solution)/shard_map/add | solution.py:70
  (8 shorter events, 0.2 us)
Async XLA Ops:
  0.0 42.8 %copy-start.2 = (s32[16]{0:T(128)S(1)}, s32[16]{0:T(128)}, u32[]{:S(2)}) copy-start(s32[16]{0:T(128)} %param.8) | copy-start | bytes 196
  1.7 43.1 %collective-permute-start = (f32[1,3,4,1,512]{4,3,2,1,0:T(1,128)}, f32[1,3,4,1,512]{4,3,2,1,0:T(1,128)}, u32[]{:S(2)}, u32[]{:S(2)}) collective-permute-start(f32[1,3,4,1,512]{4,3,2,1,0:T(1,128)} %get-tuple-element.21), channel_id=1, source_target_pairs={{0,1},{1,2},{2,3},{4,5},{5,6},{6,7},{8,9},{9,10},{10,11},{12,13},{... | collective-permute-start | bytes 73736 | tf_op jit(solution)/shard_map/ppermute | solution.py:24
  7.2 37.6 %collective-permute-start.1 = (f32[1,3,4,1,512]{4,3,2,1,0:T(1,128)}, f32[1,3,4,1,512]{4,3,2,1,0:T(1,128)}, u32[]{:S(2)}, u32[]{:S(2)}) collective-permute-start(f32[1,3,4,1,512]{4,3,2,1,0:T(1,128)} %get-tuple-element.22), channel_id=1, source_target_pairs={{1,0},{2,1},{3,2},{5,4},{6,5},{7,6},{9,8},{10,9},{11,10},{13,12},{... | collective-permute-start | bytes 73736 | tf_op jit(solution)/shard_map/ppermute | solution.py:27
  9.9 36.3 %collective-permute-start.2 = (f32[4,1,512]{2,1,0:T(1,128)}, f32[4,1,512]{2,1,0:T(1,128)S(1)}, u32[]{:S(2)}, u32[]{:S(2)}) collective-permute-start(f32[4,1,512]{2,1,0:T(1,128)} %slice.122), channel_id=1, source_target_pairs={{1,0},{2,1},{3,2},{5,4},{6,5},{7,6},{9,8},{10,9},{11,10},{13,12},{... | collective-permute-start | bytes 24584 | tf_op jit(solution)/shard_map/ppermute | solution.py:16
  23.7 21.1 %copy-start.1 = (f32[1,3,4,96,512]{4,3,2,1,0:T(8,128)S(1)}, f32[1,3,4,96,512]{4,3,2,1,0:T(8,128)}, u32[]{:S(2)}) copy-start(f32[1,3,4,96,512]{4,3,2,1,0:T(8,128)} %param.5) | copy-start | bytes 7077892
  45.9 1.1 %copy-start = (f32[4,96,512]{2,1,0:T(8,128)S(1)}, f32[4,96,512]{2,1,0:T(8,128)}, u32[]{:S(2)}) copy-start(f32[4,96,512]{2,1,0:T(8,128)} %param.6) | copy-start | bytes 2359300
  49.6 5.0 %collective-permute-start.3 = (f32[1,3,4,1,512]{4,3,2,1,0:T(1,128)S(1)}, f32[1,3,4,1,512]{4,3,2,1,0:T(1,128)S(1)}, u32[]{:S(2)}, u32[]{:S(2)}) collective-permute-start(f32[1,3,4,1,512]{4,3,2,1,0:T(1,128)S(1)} %get-tuple-element.17), channel_id=1, source_target_pairs={{0,1},{1,2},{2,3},{4,5},{5,6},{6,7},{8,9},{9,10},{10,11},{12,13},{... | collective-permute-start | bytes 73736 | tf_op jit(solution)/shard_map/ppermute | solution.py:24
  53.1 5.7 %collective-permute-start.4 = (f32[1,3,4,1,512]{4,3,2,1,0:T(1,128)S(1)}, f32[1,3,4,1,512]{4,3,2,1,0:T(1,128)S(1)}, u32[]{:S(2)}, u32[]{:S(2)}) collective-permute-start(f32[1,3,4,1,512]{4,3,2,1,0:T(1,128)S(1)} %get-tuple-element.18), channel_id=1, source_target_pairs={{1,0},{2,1},{3,2},{5,4},{6,5},{7,6},{9,8},{10,9},{11,10},{13,12},{... | collective-permute-start | bytes 73736 | tf_op jit(solution)/shard_map/ppermute | solution.py:27
  62.0 4.9 %collective-permute-start.5 = (f32[1,3,4,1,512]{4,3,2,1,0:T(1,128)S(1)}, f32[1,3,4,1,512]{4,3,2,1,0:T(1,128)S(1)}, u32[]{:S(2)}, u32[]{:S(2)}) collective-permute-start(f32[1,3,4,1,512]{4,3,2,1,0:T(1,128)S(1)} %get-tuple-element.13), channel_id=1, source_target_pairs={{0,1},{1,2},{2,3},{4,5},{5,6},{6,7},{8,9},{9,10},{10,11},{12,13},{... | collective-permute-start | bytes 73736 | tf_op jit(solution)/shard_map/ppermute | solution.py:24
  65.0 5.7 %collective-permute-start.6 = (f32[1,3,4,1,512]{4,3,2,1,0:T(1,128)S(1)}, f32[1,3,4,1,512]{4,3,2,1,0:T(1,128)S(1)}, u32[]{:S(2)}, u32[]{:S(2)}) collective-permute-start(f32[1,3,4,1,512]{4,3,2,1,0:T(1,128)S(1)} %get-tuple-element.14), channel_id=1, source_target_pairs={{1,0},{2,1},{3,2},{5,4},{6,5},{7,6},{9,8},{10,9},{11,10},{13,12},{... | collective-permute-start | bytes 73736 | tf_op jit(solution)/shard_map/ppermute | solution.py:27
where the time goes:
time: 75.7 us; the launch traced here: 75.2 us
  blocking collectives  29 us (38%)
  starting transfers between devices  17.3 us (23%)
  other arithmetic  9.96 us (13%)
  local copies, waits for them, and re-layouts  7.99 us (11%)
  waiting for transfers between devices  7.96 us (11%)
  matrix products  1.96 us (3%)
  between operations  1.01 us (1%)
    all_gather x1, blocking collectives, body(): driver_all = lax.all_gather(driver_piece, 'tile', axis=0, tiled=True)  18.1 us
    ppermute x3, starting transfers between devices, with_halo(): lax.ppermute(lax.slice_in_dim(block, block.shape[dim] - width, None, axis...  11.9 us
    all_gather x1, blocking collectives, body(): driver_piece = lax.all_gather(driver, 'member', axis=2, tiled=True)  11 us
    ppermute x3, waiting for transfers between devices, with_halo(): lax.ppermute(lax.slice_in_dim(block, 0, width, axis=dim), axis, backward)  7.95 us
    ppermute x3, starting transfers between devices, with_halo(): lax.ppermute(lax.slice_in_dim(block, 0, width, axis=dim), axis, backward)  4.04 us
    add x3, other arithmetic, advance(): return stacked + weights * (targets - stacked)  3.72 us
    select_n x3, other arithmetic, advance(): pressure = jnp.where(inside, pressure, jnp.float32(0.0))  2.12 us
    dot_general x1, matrix products, zone_geometry(): jnp.einsum('rz,zcy->cry', selector, driver_all, precision=lax.Precision.H...  1.96 us
  transfers between devices with their start and end apart: 7, of which 2 were waited for; matrix products, arithmetic and copies ran while one was open for 10% of the time, Pallas kernels for 0%

commit v1 on v0

v1 whole, which is shorter than its diff:
```python
import functools

import jax
import jax.numpy as jnp
from jax import lax
from jax.experimental import pallas as pl
from jax.experimental.pallas import tpu as pltpu
from jax.sharding import PartitionSpec as P

ZONE = 8
SUBSTEPS = 3
HALO = 3
TILE = 8
LANES = 128

relax_peak = 0.9


def rotated(field, amount, axis):
    return pltpu.roll(field, amount % field.shape[axis], axis)


def sweep(load, emit, tiles, relax, keep):
    columns = None
    pending = [None] * SUBSTEPS

    def finish(stage, above):
        index, stiff, new_pressure, along_x, new_y = pending[stage]
        row = lax.broadcasted_iota(jnp.int32, new_pressure.shape, 0)
        turned = rotated(new_pressure, -1, 0)
        if above is not None:
            turned = jnp.where(row == TILE - 1, rotated(above, -1, 0), turned)
        new_x = along_x - (turned - new_pressure)
        fields = [new_pressure, new_x, new_y]
        if relax is not None and index == 1:
            weight, targets = relax
            fields = [f + weight * (b - f) for f, b in zip(fields, targets)]
        if keep is not None and index == 0:
            fields[1] = fields[1] * keep
        push(stage + 1, index, stiff, fields)

    def push(stage, index, stiff, fields):
        if stage == SUBSTEPS:
            emit(index, fields)
            return
        pressure, along_x, along_y = fields
        row = lax.broadcasted_iota(jnp.int32, pressure.shape, 0)
        turned = rotated(along_x, 1, 0)
        before = pending[stage]
        if before is not None:
            turned = jnp.where(row == 0, rotated(before[3], 1, 0), turned)
        flow = (along_x - turned) + (along_y - rotated(along_y, 1, 1))
        new_pressure = pressure - stiff * flow
        new_y = along_y - (rotated(new_pressure, -1, 1) - new_pressure)
        if before is not None:
            finish(stage, new_pressure)
        pending[stage] = (index, stiff, new_pressure, along_x, new_y)

    for index in range(tiles):
        stiff, fields = load(index)
        push(0, index, stiff, fields)
    for stage in range(SUBSTEPS):
        finish(stage, None)


def kernel(members, tiles, zone_rows, zone_depth, state, stiffness, driver, out,
           fields, stiff, pieces, zone, load_sem, stiff_sem,
           up_send, up_recv, down_send, down_recv, piece_send, piece_recv, zone_send, zone_recv):
    levels, rows, columns = stiffness.shape
    _, parts, width = driver.shape
    per_group = LANES // width
    groups = members // per_group
    sources = tiles // 2
    per_source = driver.shape[0]
    member = lax.axis_index("member")
    tile = lax.axis_index("tile")
    bottom = tile == 0
    top = tile == tiles - 1
    edge = jnp.logical_or(bottom, top)
    group = member // per_group
    lane = member % per_group

    def at(member_to, tile_to):
        return {"member": member_to, "tile": tile_to}

    def loads(level):
        return pltpu.make_async_copy(
            state.at[0, :, level], fields.at[:, level, pl.ds(TILE, rows)], load_sem.at[level])

    stiff_load = pltpu.make_async_copy(stiffness, stiff.at[:, pl.ds(TILE, rows)], stiff_sem)

    barrier = pltpu.get_barrier_semaphore()

    def greet(device):
        pl.semaphore_signal(barrier, inc=1, device_id=device, device_id_type=pl.DeviceIdType.MESH)

    @pl.when(tile > 0)
    def _():
        greet(at(member, tile - 1))

    @pl.when(tile < tiles - 1)
    def _():
        greet(at(member, tile + 1))

    @pl.when(edge)
    def _():
        first = jnp.where(bottom, sources, 0)
        for s in range(sources):
            for g in range(per_group):
                greet(at(group * per_group + g, first + s))
        for j in range(1, groups):
            greet(at(lax.rem(group + j, groups) * per_group + lane, tile))

    stiff_load.start()
    for level in range(levels):
        loads(level).start()

    @pl.when(bottom)
    def _():
        fields[:, :, :TILE, :] = jnp.zeros((3, levels, TILE, columns), jnp.float32)
        stiff[:, :TILE, :] = jnp.zeros((levels, TILE, columns), jnp.float32)

    @pl.when(top)
    def _():
        fields[:, :, TILE + rows:, :] = jnp.zeros((3, levels, TILE, columns), jnp.float32)
        stiff[:, TILE + rows:, :] = jnp.zeros((levels, TILE, columns), jnp.float32)

    @pl.when(jnp.logical_not(edge))
    def _():
        zone[...] = jnp.zeros(zone.shape, jnp.float32)

    expected = per_group + jnp.where(bottom, 0, 1) + jnp.where(top, 0, 1)
    expected = expected + jnp.where(edge, groups - 1, 0)
    pl.semaphore_wait(barrier, expected)

    def remote(source, target, send, recv, device):
        return pltpu.make_async_remote_copy(
            src_ref=source, dst_ref=target, send_sem=send, recv_sem=recv,
            device_id=device, device_id_type=pl.DeviceIdType.MESH)

    def ups():
        device = at(member, tile + 1)
        copies = []
        for field, count in ((0, HALO - 1), (1, HALO), (2, HALO - 1)):
            copies.append(remote(
                state.at[0, field, :, pl.ds(rows - count, count)],
                fields.at[field, :, pl.ds(TILE - count, count)],
                up_send.at[field], up_recv.at[field], device))
        count = HALO - 1
        copies.append(remote(
            stiffness.at[:, pl.ds(rows - count, count)], stiff.at[:, pl.ds(TILE - count, count)],
            up_send.at[3], up_recv.at[3], device))
        return copies

    def downs():
        device = at(member, tile - 1)
        return [
            remote(state.at[0, :, :, pl.ds(0, HALO)], fields.at[:, :, pl.ds(TILE + rows, HALO)],
                   down_send.at[0], down_recv.at[0], device),
            remote(stiffness.at[:, pl.ds(0, HALO)], stiff.at[:, pl.ds(TILE + rows, HALO)],
                   down_send.at[1], down_recv.at[1], device),
        ]

    def piece(g, source_slot, lane_slot):
        target = jnp.where(tile < sources, tiles - 1, 0)
        return remote(driver, pieces.at[source_slot, lane_slot], piece_send.at[g],
                      piece_recv.at[source_slot, lane_slot], at(group * per_group + g, target))

    def zone_copy(j, slot):
        device = at(lax.rem(group + j, groups) * per_group + lane, tile)
        return remote(zone.at[slot], zone.at[slot], zone_send.at[j - 1], zone_recv.at[slot], device)

    my_slot = lax.rem(tile, sources)
    for g in range(per_group):
        piece(g, my_slot, lane).start()

    @pl.when(tile < tiles - 1)
    def _():
        for copy in ups():
            copy.start()

    @pl.when(tile > 0)
    def _():
        for copy in downs():
            copy.start()

    stiff_load.wait()

    def interior(level, carry):
        loads(level).wait()

        def load(index):
            at_rows = pl.ds(2 * TILE + TILE * index, TILE)
            return stiff[level, at_rows, :], [fields[f, level, at_rows, :] for f in range(3)]

        def emit(index, values):
            for f in range(3):
                out[0, f, level, pl.ds(TILE + TILE * index, TILE), :] = values[f]

        sweep(load, emit, rows // TILE - 2, None, None)
        return carry

    split = levels // 2
    lax.fori_loop(0, split, interior, 0)

    @pl.when(edge)
    def _():
        first = jnp.where(bottom, ZONE, 0)
        row = lax.broadcasted_iota(jnp.int32, (TILE, LANES), 0)
        wanted = jnp.where(bottom, row, 2 * ZONE - 1 - row)
        for s in range(sources):
            for g in range(per_group):
                piece(0, s, g).wait_recv()
        held = [jnp.zeros((TILE, LANES), jnp.float32) for _ in range(parts)]
        for s in range(sources):
            for r in range(per_source):
                chosen = wanted == zone_rows[first + s * per_source + r]
                block = jnp.concatenate([pieces[s, g, r] for g in range(per_group)], axis=-1)
                for part in range(parts):
                    held[part] = jnp.where(chosen, block[part:part + 1, :], held[part])
        for part in range(parts):
            zone[group, part] = held[part]
        for j in range(1, groups):
            zone_copy(j, group).start()

    lax.fori_loop(split, levels, interior, 0)

    row = lax.broadcasted_iota(jnp.int32, (TILE, columns), 0)
    depth = zone_depth[0].astype(jnp.float32)

    def weights(distance, here):
        distance = distance.astype(jnp.float32)
        ratio = (depth - distance) / depth
        return jnp.where(jnp.logical_and(here, distance < depth), relax_peak * ratio * ratio, 0.0)

    low_weight = weights(row, bottom)
    high_weight = weights(ZONE - 1 - row, top)
    keep = jnp.where(bottom, 0.0, 1.0).astype(jnp.float32)

    @pl.when(tile > 0)
    def _():
        for copy in ups():
            copy.wait_recv()

    @pl.when(tile < tiles - 1)
    def _():
        for copy in downs():
            copy.wait_recv()

    @pl.when(edge)
    def _():
        for j in range(1, groups):
            zone_copy(j, lax.rem(group + groups - j, groups)).wait_recv()

    def strips(level, carry):
        def targets():
            return [jnp.concatenate([zone[g, f * levels + level] for g in range(groups)], axis=-1)
                    for f in range(3)]

        def strip(base, weight, keep, emit):
            def load(index):
                at_rows = pl.ds(base + TILE * index, TILE)
                return stiff[level, at_rows, :], [fields[f, level, at_rows, :] for f in range(3)]

            sweep(load, emit, 3, (weight, targets()), keep)

        def emit_low(index, values):
            for f in range(3):
                if index == 1:
                    out[0, f, level, pl.ds(0, TILE), :] = values[f]
                if index == 2:
                    out[0, f, level, pl.ds(TILE, HALO), :] = values[f][:HALO]

        def emit_high(index, values):
            for f in range(3):
                if index == 0:
                    out[0, f, level, pl.ds(rows - TILE - HALO, HALO), :] = values[f][TILE - HALO:]
                if index == 1:
                    out[0, f, level, pl.ds(rows - TILE, TILE), :] = values[f]

        strip(0, low_weight, keep, emit_low)
        strip(rows - TILE, high_weight, None, emit_high)
        return carry

    lax.fori_loop(0, levels, strips, 0)

    @pl.when(tile < tiles - 1)
    def _():
        for copy in ups():
            copy.wait_send()

    @pl.when(tile > 0)
    def _():
        for copy in downs():
            copy.wait_send()

    for g in range(per_group):
        piece(g, my_slot, lane).wait_send()

    @pl.when(edge)
    def _():
        for j in range(1, groups):
            zone_copy(j, group).wait_send()


def body(state, stiffness, driver, zone_rows, zone_depth):
    members = lax.axis_size("member")
    tiles = lax.axis_size("tile")
    levels, rows, columns = stiffness.shape
    parts, width = driver.shape[1:]
    per_group = LANES // width
    groups = members // per_group
    dma = pltpu.SemaphoreType.DMA
    padded = rows + 2 * TILE
    return pl.pallas_call(
        functools.partial(kernel, members, tiles),
        out_shape=jax.ShapeDtypeStruct(state.shape, jnp.float32),
        in_specs=[pl.BlockSpec(memory_space=pltpu.SMEM)] * 2
        + [pl.BlockSpec(memory_space=pl.ANY)] * 3,
        out_specs=pl.BlockSpec(memory_space=pltpu.VMEM),
        scratch_shapes=[
            pltpu.VMEM((3, levels, padded, columns), jnp.float32),
            pltpu.VMEM((levels, padded, columns), jnp.float32),
            pltpu.VMEM((tiles // 2, per_group) + driver.shape, jnp.float32),
            pltpu.VMEM((groups, parts, TILE, LANES), jnp.float32),
            dma((levels,)),
            dma,
            dma((4,)),
            dma((4,)),
            dma((2,)),
            dma((2,)),
            dma((per_group,)),
            dma((tiles // 2, per_group)),
            dma((groups,)),
            dma((groups,)),
        ],
        compiler_params=pltpu.CompilerParams(
            collective_id=0, has_side_effects=True, vmem_limit_bytes=40 * 2**20),
        name="substeps",
    )(zone_rows, zone_depth, state, stiffness, driver)


def solution(mesh):
    in_specs = (
        P("member", None, None, "tile", None),
        P(None, "tile", None),
        P("tile", None, "member"),
        P(),
        P("member"),
    )
    out_specs = P("member", None, None, "tile", None)
    return jax.shard_map(body, mesh=mesh, in_specs=in_specs, out_specs=out_specs, check_vma=False)
```

time: 75.7 us -> 23 us (0.30)
  blocking collectives: 29 us -> 0 us
  starting transfers between devices: 17.3 us -> 0 us
  Pallas kernels: 0 us -> 16.4 us
  other arithmetic: 9.96 us -> 0 us
  waiting for transfers between devices: 7.96 us -> 0 us
  local copies, waits for them, and re-layouts: 7.99 us -> 5.6 us
  matrix products: 1.96 us -> 0 us
    all_gather x2 -> x0, blocking collectives: 29 us -> none  [the longest x1 18.1 us: body(): driver_all = lax.all_gather(driver_piece, 'tile', axis=0, tiled=True)]
    ppermute x7 -> x0, starting transfers between devices: 17.3 us -> none  [the longest x3 11.9 us: with_halo(): lax.ppermute(lax.slice_in_dim(block, block.shape[dim] - width, None, axis...]
    pallas_call x0 -> x1, Pallas kernels: none -> 16.4 us  [body(): pl.pallas_call(functools.partial(kernel, members, tiles), out_shape=jax.S...]
    ppermute x7 -> x0, waiting for transfers between devices: 7.96 us -> none  [the longest x3 7.95 us: with_halo(): lax.ppermute(lax.slice_in_dim(block, 0, width, axis=dim), axis, backward)]
    slice x19 -> x0, local copies, waits for them, and re-layouts: 5.5 us -> none  [the longest x3 1.77 us: with_halo(): lax.slice_in_dim(block, block.shape[dim] - width, None, axis=dim)]
    unnamed x7 -> x8, local copies, waits for them, and re-layouts: 1.71 us -> 5.6 us
    add x3 -> x0, other arithmetic: 3.72 us -> none  [advance(): return stacked + weights * (targets - stacked)]
    select_n x5 -> x0, other arithmetic: 2.74 us -> none  [the longest x3 2.12 us: advance(): pressure = jnp.where(inside, pressure, jnp.float32(0.0))]
  transfers between devices with their start and end apart: 7 -> 0, of which waited for: 2 -> 0; matrix products, arithmetic and copies ran while one was open for 10% -> 0% of each run, Pallas kernels for 0% -> 0%
where the time goes in v1:
time: 23 us; the launch traced here: 22.7 us
  Pallas kernels  16.4 us (71%)
  local copies, waits for them, and re-layouts  5.6 us (24%)
  between operations  0.66 us (3%)
    pallas_call x1, Pallas kernels, body(): pl.pallas_call(functools.partial(kernel, members, tiles), out_shape=jax.S...  16.4 us
    unnamed x8, local copies, waits for them, and re-layouts  5.6 us

profile of v1, /device:TPU:0, one launch (start us, length us, event | category | flops | bytes accessed | tf_op | source)
XLA Modules:
  0.0 22.7 jit_solution(11921343646154151177)
XLA Ops:
  0.7 0.7 %copy.6.driver = f32[4,12,64]{2,1,0:T(8,128)S(1)} copy(f32[4,12,64]{2,0,1:T(4,128)} %param.7) | data formatting | bytes 24576 | tf_op args[2]
  1.4 0.0 copy-start
  1.4 1.7 %copy-done = f32[1,3,4,96,512]{4,3,2,1,0:T(8,128)S(1)} copy-done((f32[1,3,4,96,512]{4,3,2,1,0:T(8,128)S(1)}, f32[1,3,4,96,512]{4,3,2,1,0:T(8,128)}, u32[]{:S(2)}) %copy-start) | copy-done | bytes 2359320
  3.1 0.0 copy-start.1
  3.1 1.1 %copy-done.1 = f32[4,96,512]{2,1,0:T(8,128)S(1)} copy-done((f32[4,96,512]{2,1,0:T(8,128)S(1)}, f32[4,96,512]{2,1,0:T(8,128)}, u32[]{:S(2)}) %copy-start.1) | copy-done | bytes 786456
  4.2 0.0 copy-start.2
  4.2 0.7 %copy-done.2 = s32[16]{0:T(128)S(1)} copy-done((s32[16]{0:T(128)S(1)}, s32[16]{0:T(128)}, u32[]{:S(2)}) %copy-start.2) | copy-done | bytes 88
  4.8 16.4 %substeps.1 = f32[1,3,4,96,512]{4,3,2,1,0:T(8,128)S(1)} custom-call(s32[16]{0:T(128)S(1)} %copy-done.2, s32[1]{0:T(128)S(6)} %copy.8.zone_depth, f32[1,3,4,96,512]{4,3,2,1,0:T(8,128)S(1)} %copy-done, f32[4,96,512]{2,1,0:T(8,128)S(1)} %copy-done.1, f32[4,12,64]{2,1,0:T(8,128)S(1)} %copy.6.driver), custom_call_target="tpu_custom_call" | custom-call | tf_op jit(solution)/shard_map/substeps/pallas_call | solution.py:315
  21.3 1.4 %copy.9 = f32[1,3,4,96,512]{4,3,2,1,0:T(8,128)} copy(f32[1,3,4,96,512]{4,3,2,1,0:T(8,128)S(1)} %substeps.1) | data formatting | bytes 4718592
Async XLA Ops:
  1.4 1.7 %copy-start = (f32[1,3,4,96,512]{4,3,2,1,0:T(8,128)S(1)}, f32[1,3,4,96,512]{4,3,2,1,0:T(8,128)}, u32[]{:S(2)}) copy-start(f32[1,3,4,96,512]{4,3,2,1,0:T(8,128)} %state.1) | copy-start | bytes 7077892
  3.1 1.1 %copy-start.1 = (f32[4,96,512]{2,1,0:T(8,128)S(1)}, f32[4,96,512]{2,1,0:T(8,128)}, u32[]{:S(2)}) copy-start(f32[4,96,512]{2,1,0:T(8,128)} %stiffness.1) | copy-start | bytes 2359300
  4.2 0.7 %copy-start.2 = (s32[16]{0:T(128)S(1)}, s32[16]{0:T(128)}, u32[]{:S(2)}) copy-start(s32[16]{0:T(128)} %zone_rows.1) | copy-start | bytes 196

commit v2 on v1

--- a/solution.py
+++ b/solution.py
@@ -63,15 +63,14 @@
         finish(stage, None)
 
 
-def kernel(members, tiles, zone_rows, zone_depth, state, stiffness, driver, out,
-           fields, stiff, pieces, zone, load_sem, stiff_sem,
+def kernel(members, tiles, zone_depth, zone_rows_hbm, state, stiffness, driver, out,
+           zone_rows, rows_sem, fields, stiff, pieces, zone, load_sem, stiff_sem,
            up_send, up_recv, down_send, down_recv, piece_send, piece_recv, zone_send, zone_recv):
     levels, rows, columns = stiffness.shape
-    _, parts, width = driver.shape
+    parts, per_source, width = driver.shape
     per_group = LANES // width
     groups = members // per_group
     sources = tiles // 2
-    per_source = driver.shape[0]
     member = lax.axis_index("member")
     tile = lax.axis_index("tile")
     bottom = tile == 0
@@ -111,9 +110,11 @@
         for j in range(1, groups):
             greet(at(lax.rem(group + j, groups) * per_group + lane, tile))
 
+    rows_load = pltpu.make_async_copy(zone_rows_hbm, zone_rows, rows_sem)
     stiff_load.start()
     for level in range(levels):
         loads(level).start()
+    rows_load.start()
 
     @pl.when(bottom)
     def _():
@@ -185,6 +186,7 @@
             copy.start()
 
     stiff_load.wait()
+    rows_load.wait()
 
     def interior(level, carry):
         loads(level).wait()
@@ -213,11 +215,11 @@
                 piece(0, s, g).wait_recv()
         held = [jnp.zeros((TILE, LANES), jnp.float32) for _ in range(parts)]
         for s in range(sources):
-            for r in range(per_source):
-                chosen = wanted == zone_rows[first + s * per_source + r]
-                block = jnp.concatenate([pieces[s, g, r] for g in range(per_group)], axis=-1)
-                for part in range(parts):
-                    held[part] = jnp.where(chosen, block[part:part + 1, :], held[part])
+            chosen = [wanted == zone_rows[first + s * per_source + r] for r in range(per_source)]
+            for part in range(parts):
+                block = jnp.concatenate([pieces[s, g, part] for g in range(per_group)], axis=-1)
+                for r in range(per_source):
+                    held[part] = jnp.where(chosen[r], block[r:r + 1, :], held[part])
         for part in range(parts):
             zone[group, part] = held[part]
         for j in range(1, groups):
@@ -307,18 +309,23 @@
     members = lax.axis_size("member")
     tiles = lax.axis_size("tile")
     levels, rows, columns = stiffness.shape
-    parts, width = driver.shape[1:]
+    driver = jnp.transpose(driver, (1, 0, 2))
+    parts, _, width = driver.shape
     per_group = LANES // width
     groups = members // per_group
     dma = pltpu.SemaphoreType.DMA
     padded = rows + 2 * TILE
+    operands = [pltpu.with_memory_space_constraint(operand, pltpu.HBM)
+                for operand in (zone_rows, state, stiffness, driver)]
     return pl.pallas_call(
         functools.partial(kernel, members, tiles),
         out_shape=jax.ShapeDtypeStruct(state.shape, jnp.float32),
-        in_specs=[pl.BlockSpec(memory_space=pltpu.SMEM)] * 2
-        + [pl.BlockSpec(memory_space=pl.ANY)] * 3,
+        in_specs=[pl.BlockSpec(memory_space=pltpu.SMEM)]
+        + [pl.BlockSpec(memory_space=pltpu.HBM)] * 4,
         out_specs=pl.BlockSpec(memory_space=pltpu.VMEM),
         scratch_shapes=[
+            pltpu.SMEM(zone_rows.shape, jnp.int32),
+            dma,
             pltpu.VMEM((3, levels, padded, columns), jnp.float32),
             pltpu.VMEM((levels, padded, columns), jnp.float32),
             pltpu.VMEM((tiles // 2, per_group) + driver.shape, jnp.float32),
@@ -337,7 +344,7 @@
         compiler_params=pltpu.CompilerParams(
             collective_id=0, has_side_effects=True, vmem_limit_bytes=40 * 2**20),
         name="substeps",
-    )(zone_rows, zone_depth, state, stiffness, driver)
+    )(zone_depth, *operands)
 
 
 def solution(mesh):

time: 23 us -> 18.3 us (0.80)
  local copies, waits for them, and re-layouts: 5.6 us -> 1.41 us
  Pallas kernels: 16.4 us -> 16.1 us
    unnamed x8 -> x1, local copies, waits for them, and re-layouts: 5.6 us -> 1.41 us
    pallas_call x1, Pallas kernels: 16.4 us -> 16.1 us  [body(): pl.pallas_call(functools.partial(kernel, members, tiles), out_shape=jax.S...]
where the time goes in v2:
time: 18.3 us; the launch traced here: 18.2 us
  Pallas kernels  16.1 us (88%)
  local copies, waits for them, and re-layouts  1.41 us (8%)
  between operations  0.66 us (4%)
    pallas_call x1, Pallas kernels, body(): pl.pallas_call(functools.partial(kernel, members, tiles), out_shape=jax.S...  16.1 us
    unnamed x1, local copies, waits for them, and re-layouts  1.41 us

profile of v2, /device:TPU:0, one launch (start us, length us, event | category | flops | bytes accessed | tf_op | source)
XLA Modules:
  0.0 18.2 jit_solution(7409750283682552512)
XLA Ops:
  0.7 16.1 %substeps.1 = f32[1,3,4,96,512]{4,3,2,1,0:T(8,128)S(1)} custom-call(s32[1]{0:T(128)S(6)} %copy.7.zone_depth, s32[16]{0:T(128)} %zone_rows_hbm.1, f32[1,3,4,96,512]{4,3,2,1,0:T(8,128)} %state.1, f32[4,96,512]{2,1,0:T(8,128)} %stiffness.1, f32[12,4,64]{2,1,0:T(4,128)} %bitcast.1), custom_call_target="tpu_custom_call" | custom-call | tf_op jit(solution)/shard_map/substeps/pallas_call | solution.py:320
  16.8 1.4 %copy.8 = f32[1,3,4,96,512]{4,3,2,1,0:T(8,128)} copy(f32[1,3,4,96,512]{4,3,2,1,0:T(8,128)S(1)} %substeps.1) | data formatting | bytes 4718592

commit v3 on v2

--- a/solution.py
+++ b/solution.py
@@ -64,7 +64,8 @@
 
 
 def kernel(members, tiles, zone_depth, zone_rows_hbm, state, stiffness, driver, out,
-           zone_rows, rows_sem, fields, stiff, pieces, zone, load_sem, stiff_sem,
+           zone_rows, rows_sem, fields, stiff, own, packed, pieces, zone,
+           load_sem, stiff_sem, own_sem,
            up_send, up_recv, down_send, down_recv, piece_send, piece_recv, zone_send, zone_recv):
     levels, rows, columns = stiffness.shape
     parts, per_source, width = driver.shape
@@ -110,7 +111,9 @@
         for j in range(1, groups):
             greet(at(lax.rem(group + j, groups) * per_group + lane, tile))
 
+    own_load = pltpu.make_async_copy(driver, own, own_sem)
     rows_load = pltpu.make_async_copy(zone_rows_hbm, zone_rows, rows_sem)
+    own_load.start()
     stiff_load.start()
     for level in range(levels):
         loads(level).start()
@@ -130,6 +133,12 @@
     def _():
         zone[...] = jnp.zeros(zone.shape, jnp.float32)
 
+    half = parts // 2
+    own_load.wait()
+    for part in range(half):
+        packed[pl.ds(part * per_source, per_source), :] = jnp.concatenate(
+            [own[part], own[part + half]], axis=-1)
+
     expected = per_group + jnp.where(bottom, 0, 1) + jnp.where(top, 0, 1)
     expected = expected + jnp.where(edge, groups - 1, 0)
     pl.semaphore_wait(barrier, expected)
@@ -139,58 +148,65 @@
             src_ref=source, dst_ref=target, send_sem=send, recv_sem=recv,
             device_id=device, device_id_type=pl.DeviceIdType.MESH)
 
-    def ups():
-        device = at(member, tile + 1)
-        copies = []
-        for field, count in ((0, HALO - 1), (1, HALO), (2, HALO - 1)):
-            copies.append(remote(
-                state.at[0, field, :, pl.ds(rows - count, count)],
-                fields.at[field, :, pl.ds(TILE - count, count)],
-                up_send.at[field], up_recv.at[field], device))
-        count = HALO - 1
-        copies.append(remote(
-            stiffness.at[:, pl.ds(rows - count, count)], stiff.at[:, pl.ds(TILE - count, count)],
-            up_send.at[3], up_recv.at[3], device))
-        return copies
-
-    def downs():
-        device = at(member, tile - 1)
-        return [
-            remote(state.at[0, :, :, pl.ds(0, HALO)], fields.at[:, :, pl.ds(TILE + rows, HALO)],
-                   down_send.at[0], down_recv.at[0], device),
-            remote(stiffness.at[:, pl.ds(0, HALO)], stiff.at[:, pl.ds(TILE + rows, HALO)],
-                   down_send.at[1], down_recv.at[1], device),
-        ]
+    count = HALO - 1
+
+    def stiff_up():
+        return remote(stiff.at[:, pl.ds(TILE + rows - count, count)],
+                      stiff.at[:, pl.ds(TILE - count, count)],
+                      up_send.at[levels], up_recv.at[levels], at(member, tile + 1))
+
+    def stiff_down():
+        return remote(stiff.at[:, pl.ds(TILE, HALO)], stiff.at[:, pl.ds(TILE + rows, HALO)],
+                      down_send.at[levels], down_recv.at[levels], at(member, tile - 1))
+
+    def up(level):
+        return remote(fields.at[:, level, pl.ds(TILE + rows - HALO, HALO)],
+                      fields.at[:, level, pl.ds(TILE - HALO, HALO)],
+                      up_send.at[level], up_recv.at[level], at(member, tile + 1))
+
+    def down(level):
+        return remote(fields.at[:, level, pl.ds(TILE, HALO)],
+                      fields.at[:, level, pl.ds(TILE + rows, HALO)],
+                      down_send.at[level], down_recv.at[level], at(member, tile - 1))
 
     def piece(g, source_slot, lane_slot):
         target = jnp.where(tile < sources, tiles - 1, 0)
-        return remote(driver, pieces.at[source_slot, lane_slot], piece_send.at[g],
+        return remote(packed, pieces.at[source_slot, lane_slot], piece_send.at[g],
                       piece_recv.at[source_slot, lane_slot], at(group * per_group + g, target))
 
-    def zone_copy(j, slot):
+    def zone_copy(j, level, slot):
         device = at(lax.rem(group + j, groups) * per_group + lane, tile)
-        return remote(zone.at[slot], zone.at[slot], zone_send.at[j - 1], zone_recv.at[slot], device)
+        return remote(zone.at[slot, level], zone.at[slot, level], zone_send.at[level, j - 1],
+                      zone_recv.at[level, slot], device)
 
     my_slot = lax.rem(tile, sources)
     for g in range(per_group):
         piece(g, my_slot, lane).start()
 
+    stiff_load.wait()
+
     @pl.when(tile < tiles - 1)
     def _():
-        for copy in ups():
-            copy.start()
+        stiff_up().start()
 
     @pl.when(tile > 0)
     def _():
-        for copy in downs():
-            copy.start()
-
-    stiff_load.wait()
+        stiff_down().start()
+
+    for level in range(levels):
+        loads(level).wait()
+
+        @pl.when(tile < tiles - 1)
+        def _():
+            up(level).start()
+
+        @pl.when(tile > 0)
+        def _():
+            down(level).start()
+
     rows_load.wait()
 
     def interior(level, carry):
-        loads(level).wait()
-
         def load(index):
             at_rows = pl.ds(2 * TILE + TILE * index, TILE)
             return stiff[level, at_rows, :], [fields[f, level, at_rows, :] for f in range(3)]
@@ -202,7 +218,7 @@
         sweep(load, emit, rows // TILE - 2, None, None)
         return carry
 
-    split = levels // 2
+    split = levels // 4
     lax.fori_loop(0, split, interior, 0)
 
     @pl.when(edge)
@@ -217,13 +233,17 @@
         for s in range(sources):
             chosen = [wanted == zone_rows[first + s * per_source + r] for r in range(per_source)]
             for part in range(parts):
-                block = jnp.concatenate([pieces[s, g, part] for g in range(per_group)], axis=-1)
+                at_rows = pl.ds(part % half * per_source, per_source)
+                at_lanes = pl.ds(part // half * width, width)
+                block = jnp.concatenate(
+                    [pieces[s, g, at_rows, at_lanes] for g in range(per_group)], axis=-1)
                 for r in range(per_source):
                     held[part] = jnp.where(chosen[r], block[r:r + 1, :], held[part])
         for part in range(parts):
-            zone[group, part] = held[part]
-        for j in range(1, groups):
-            zone_copy(j, group).start()
+            zone[group, part % levels, part // levels] = held[part]
+        for level in range(levels):
+            for j in range(1, groups):
+                zone_copy(j, level, group).start()
 
     lax.fori_loop(split, levels, interior, 0)
 
@@ -241,22 +261,28 @@
 
     @pl.when(tile > 0)
     def _():
-        for copy in ups():
-            copy.wait_recv()
+        stiff_up().wait_recv()
 
     @pl.when(tile < tiles - 1)
     def _():
-        for copy in downs():
-            copy.wait_recv()
-
-    @pl.when(edge)
-    def _():
-        for j in range(1, groups):
-            zone_copy(j, lax.rem(group + groups - j, groups)).wait_recv()
+        stiff_down().wait_recv()
 
     def strips(level, carry):
+        @pl.when(tile > 0)
+        def _():
+            up(level).wait_recv()
+
+        @pl.when(tile < tiles - 1)
+        def _():
+            down(level).wait_recv()
+
+        @pl.when(edge)
+        def _():
+            for j in range(1, groups):
+                zone_copy(j, level, lax.rem(group + groups - j, groups)).wait_recv()
+
         def targets():
-            return [jnp.concatenate([zone[g, f * levels + level] for g in range(groups)], axis=-1)
+            return [jnp.concatenate([zone[g, level, f] for g in range(groups)], axis=-1)
                     for f in range(3)]
 
         def strip(base, weight, keep, emit):
@@ -288,21 +314,24 @@
 
     @pl.when(tile < tiles - 1)
     def _():
-        for copy in ups():
-            copy.wait_send()
+        stiff_up().wait_send()
+        for level in range(levels):
+            up(level).wait_send()
 
     @pl.when(tile > 0)
     def _():
-        for copy in downs():
-            copy.wait_send()
+        stiff_down().wait_send()
+        for level in range(levels):
+            down(level).wait_send()
 
     for g in range(per_group):
         piece(g, my_slot, lane).wait_send()
 
     @pl.when(edge)
     def _():
-        for j in range(1, groups):
-            zone_copy(j, group).wait_send()
+        for level in range(levels):
+            for j in range(1, groups):
+                zone_copy(j, level, group).wait_send()
 
 
 def body(state, stiffness, driver, zone_rows, zone_depth):
@@ -310,7 +339,8 @@
     tiles = lax.axis_size("tile")
     levels, rows, columns = stiffness.shape
     driver = jnp.transpose(driver, (1, 0, 2))
-    parts, _, width = driver.shape
+    parts, per_source, width = driver.shape
+    packed = (parts // 2 * per_source, 2 * width)
     per_group = LANES // width
     groups = members // per_group
     dma = pltpu.SemaphoreType.DMA
@@ -328,18 +358,21 @@
             dma,
             pltpu.VMEM((3, levels, padded, columns), jnp.float32),
             pltpu.VMEM((levels, padded, columns), jnp.float32),
-            pltpu.VMEM((tiles // 2, per_group) + driver.shape, jnp.float32),
-            pltpu.VMEM((groups, parts, TILE, LANES), jnp.float32),
+            pltpu.VMEM(driver.shape, jnp.float32),
+            pltpu.VMEM(packed, jnp.float32),
+            pltpu.VMEM((tiles // 2, per_group) + packed, jnp.float32),
+            pltpu.VMEM((groups, levels, parts // levels, TILE, LANES), jnp.float32),
             dma((levels,)),
             dma,
-            dma((4,)),
-            dma((4,)),
-            dma((2,)),
-            dma((2,)),
+            dma,
+            dma((levels + 1,)),
+            dma((levels + 1,)),
+            dma((levels + 1,)),
+            dma((levels + 1,)),
             dma((per_group,)),
             dma((tiles // 2, per_group)),
-            dma((groups,)),
-            dma((groups,)),
+            dma((levels, groups)),
+            dma((levels, groups)),
         ],
         compiler_params=pltpu.CompilerParams(
             collective_id=0, has_side_effects=True, vmem_limit_bytes=40 * 2**20),

time: 18.3 us -> 17.5 us (0.956)
  Pallas kernels: 16.1 us -> 15.3 us
    pallas_call x1, Pallas kernels: 16.1 us -> 15.3 us  [body(): pl.pallas_call(functools.partial(kernel, members, tiles), out_shape=jax.S...]
where the time goes in v3:
time: 17.5 us; the launch traced here: 17.3 us
  Pallas kernels  15.3 us (87%)
  local copies, waits for them, and re-layouts  1.41 us (8%)
  between operations  0.66 us (4%)
    pallas_call x1, Pallas kernels, body(): pl.pallas_call(functools.partial(kernel, members, tiles), out_shape=jax.S...  15.3 us
    unnamed x1, local copies, waits for them, and re-layouts  1.41 us

profile of v3, /device:TPU:0, one launch (start us, length us, event | category | flops | bytes accessed | tf_op | source)
XLA Modules:
  0.0 17.3 jit_solution(1987400890075596566)
XLA Ops:
  0.7 15.3 %substeps.1 = f32[1,3,4,96,512]{4,3,2,1,0:T(8,128)S(1)} custom-call(s32[1]{0:T(128)S(6)} %copy.7.zone_depth, s32[16]{0:T(128)} %zone_rows_hbm.1, f32[1,3,4,96,512]{4,3,2,1,0:T(8,128)} %state.1, f32[4,96,512]{2,1,0:T(8,128)} %stiffness.1, f32[12,4,64]{2,1,0:T(4,128)} %bitcast.1), custom_call_target="tpu_custom_call" | custom-call | tf_op jit(solution)/shard_map/substeps/pallas_call | solution.py:350
  15.9 1.4 %copy.8 = f32[1,3,4,96,512]{4,3,2,1,0:T(8,128)} copy(f32[1,3,4,96,512]{4,3,2,1,0:T(8,128)S(1)} %substeps.1) | data formatting | bytes 4718592

commit v4 on v3

--- a/solution.py
+++ b/solution.py
@@ -20,7 +20,7 @@
     return pltpu.roll(field, amount % field.shape[axis], axis)
 
 
-def sweep(load, emit, tiles, relax, keep):
+def sweep(load, emit, tiles, relax, outside):
     columns = None
     pending = [None] * SUBSTEPS
 
@@ -35,8 +35,8 @@
         if relax is not None and index == 1:
             weight, targets = relax
             fields = [f + weight * (b - f) for f, b in zip(fields, targets)]
-        if keep is not None and index == 0:
-            fields[1] = fields[1] * keep
+        if outside and index == 0:
+            fields[1] = jnp.zeros_like(new_x)
         push(stage + 1, index, stiff, fields)
 
     def push(stage, index, stiff, fields):
@@ -129,10 +129,6 @@
         fields[:, :, TILE + rows:, :] = jnp.zeros((3, levels, TILE, columns), jnp.float32)
         stiff[:, TILE + rows:, :] = jnp.zeros((levels, TILE, columns), jnp.float32)
 
-    @pl.when(jnp.logical_not(edge))
-    def _():
-        zone[...] = jnp.zeros(zone.shape, jnp.float32)
-
     half = parts // 2
     own_load.wait()
     for part in range(half):
@@ -174,10 +170,9 @@
         return remote(packed, pieces.at[source_slot, lane_slot], piece_send.at[g],
                       piece_recv.at[source_slot, lane_slot], at(group * per_group + g, target))
 
-    def zone_copy(j, level, slot):
+    def zone_copy(j, slot):
         device = at(lax.rem(group + j, groups) * per_group + lane, tile)
-        return remote(zone.at[slot, level], zone.at[slot, level], zone_send.at[level, j - 1],
-                      zone_recv.at[level, slot], device)
+        return remote(zone.at[slot], zone.at[slot], zone_send.at[j - 1], zone_recv.at[slot], device)
 
     my_slot = lax.rem(tile, sources)
     for g in range(per_group):
@@ -215,7 +210,7 @@
             for f in range(3):
                 out[0, f, level, pl.ds(TILE + TILE * index, TILE), :] = values[f]
 
-        sweep(load, emit, rows // TILE - 2, None, None)
+        sweep(load, emit, rows // TILE - 2, None, False)
         return carry
 
     split = levels // 4
@@ -241,9 +236,8 @@
                     held[part] = jnp.where(chosen[r], block[r:r + 1, :], held[part])
         for part in range(parts):
             zone[group, part % levels, part // levels] = held[part]
-        for level in range(levels):
-            for j in range(1, groups):
-                zone_copy(j, level, group).start()
+        for j in range(1, groups):
+            zone_copy(j, group).start()
 
     lax.fori_loop(split, levels, interior, 0)
 
@@ -257,60 +251,84 @@
 
     low_weight = weights(row, bottom)
     high_weight = weights(ZONE - 1 - row, top)
-    keep = jnp.where(bottom, 0.0, 1.0).astype(jnp.float32)
-
-    @pl.when(tile > 0)
-    def _():
-        stiff_up().wait_recv()
-
-    @pl.when(tile < tiles - 1)
-    def _():
-        stiff_down().wait_recv()
-
-    def strips(level, carry):
-        @pl.when(tile > 0)
-        def _():
-            up(level).wait_recv()
-
-        @pl.when(tile < tiles - 1)
-        def _():
-            down(level).wait_recv()
-
-        @pl.when(edge)
-        def _():
-            for j in range(1, groups):
-                zone_copy(j, level, lax.rem(group + groups - j, groups)).wait_recv()
-
-        def targets():
-            return [jnp.concatenate([zone[g, level, f] for g in range(groups)], axis=-1)
-                    for f in range(3)]
-
-        def strip(base, weight, keep, emit):
-            def load(index):
-                at_rows = pl.ds(base + TILE * index, TILE)
-                return stiff[level, at_rows, :], [fields[f, level, at_rows, :] for f in range(3)]
-
-            sweep(load, emit, 3, (weight, targets()), keep)
-
-        def emit_low(index, values):
+    def strip(level, base, weight, outside, emit):
+        def load(index):
+            at_rows = pl.ds(base + TILE * index, TILE)
+            return stiff[level, at_rows, :], [fields[f, level, at_rows, :] for f in range(3)]
+
+        relax = None
+        if weight is not None:
+            relax = (weight, [jnp.concatenate([zone[g, level, f] for g in range(groups)], axis=-1)
+                              for f in range(3)])
+        sweep(load, emit, 3, relax, outside)
+
+    def low_strip(level, weight):
+        def emit(index, values):
             for f in range(3):
                 if index == 1:
                     out[0, f, level, pl.ds(0, TILE), :] = values[f]
                 if index == 2:
                     out[0, f, level, pl.ds(TILE, HALO), :] = values[f][:HALO]
 
-        def emit_high(index, values):
+        strip(level, 0, weight, weight is not None, emit)
+
+    def high_strip(level, weight):
+        def emit(index, values):
             for f in range(3):
                 if index == 0:
                     out[0, f, level, pl.ds(rows - TILE - HALO, HALO), :] = values[f][TILE - HALO:]
                 if index == 1:
                     out[0, f, level, pl.ds(rows - TILE, TILE), :] = values[f]
 
-        strip(0, low_weight, keep, emit_low)
-        strip(rows - TILE, high_weight, None, emit_high)
-        return carry
-
-    lax.fori_loop(0, levels, strips, 0)
+        strip(level, rows - TILE, weight, False, emit)
+
+    def zone_arrival():
+        for j in range(1, groups):
+            zone_copy(j, lax.rem(group + groups - j, groups)).wait_recv()
+
+    def low_arrival(level):
+        up(level).wait_recv()
+
+    def high_arrival(level):
+        down(level).wait_recv()
+
+    def strips(together, arrivals, one):
+        def several(index, carry):
+            chosen = [index * together + k for k in range(together)]
+            for level in chosen:
+                for arrival in arrivals:
+                    arrival(level)
+            for level in chosen:
+                one(level)
+            return carry
+
+        lax.fori_loop(0, levels // together, several, 0)
+
+    pair = 2 if levels % 2 == 0 else 1
+
+    @pl.when(bottom)
+    def _():
+        stiff_down().wait_recv()
+        strips(pair, [high_arrival], lambda level: high_strip(level, None))
+        zone_arrival()
+        strips(levels, [], lambda level: low_strip(level, low_weight))
+
+    @pl.when(top)
+    def _():
+        stiff_up().wait_recv()
+        strips(pair, [low_arrival], lambda level: low_strip(level, None))
+        zone_arrival()
+        strips(levels, [], lambda level: high_strip(level, high_weight))
+
+    @pl.when(jnp.logical_not(edge))
+    def _():
+        def both(level):
+            low_strip(level, None)
+            high_strip(level, None)
+
+        stiff_up().wait_recv()
+        stiff_down().wait_recv()
+        strips(1, [low_arrival, high_arrival], both)
 
     @pl.when(tile < tiles - 1)
     def _():
@@ -329,9 +347,8 @@
 
     @pl.when(edge)
     def _():
-        for level in range(levels):
-            for j in range(1, groups):
-                zone_copy(j, level, group).wait_send()
+        for j in range(1, groups):
+            zone_copy(j, group).wait_send()
 
 
 def body(state, stiffness, driver, zone_rows, zone_depth):
@@ -371,8 +388,8 @@
             dma((levels + 1,)),
             dma((per_group,)),
             dma((tiles // 2, per_group)),
-            dma((levels, groups)),
-            dma((levels, groups)),
+            dma((groups,)),
+            dma((groups,)),
         ],
         compiler_params=pltpu.CompilerParams(
             collective_id=0, has_side_effects=True, vmem_limit_bytes=40 * 2**20),

time: 17.5 us -> 16.5 us (0.943)
  Pallas kernels: 15.3 us -> 14.3 us
    pallas_call x1, Pallas kernels: 15.3 us -> 14.3 us  [body(): pl.pallas_call(functools.partial(kernel, members, tiles), out_shape=jax.S...]
where the time goes in v4:
time: 16.5 us; the launch traced here: 16.4 us
  Pallas kernels  14.3 us (87%)
  local copies, waits for them, and re-layouts  1.41 us (9%)
  between operations  0.66 us (4%)
    pallas_call x1, Pallas kernels, body(): pl.pallas_call(functools.partial(kernel, members, tiles), out_shape=jax.S...  14.3 us
    unnamed x1, local copies, waits for them, and re-layouts  1.41 us

profile of v4, /device:TPU:0, one launch (start us, length us, event | category | flops | bytes accessed | tf_op | source)
XLA Modules:
  0.0 16.4 jit_solution(6783257816190704306)
XLA Ops:
  0.7 14.3 %substeps.1 = f32[1,3,4,96,512]{4,3,2,1,0:T(8,128)S(1)} custom-call(s32[1]{0:T(128)S(6)} %copy.7.zone_depth, s32[16]{0:T(128)} %zone_rows_hbm.1, f32[1,3,4,96,512]{4,3,2,1,0:T(8,128)} %state.1, f32[4,96,512]{2,1,0:T(8,128)} %stiffness.1, f32[12,4,64]{2,1,0:T(4,128)} %bitcast.1), custom_call_target="tpu_custom_call" | custom-call | tf_op jit(solution)/shard_map/substeps/pallas_call | solution.py:367
  15.0 1.4 %copy.8 = f32[1,3,4,96,512]{4,3,2,1,0:T(8,128)} copy(f32[1,3,4,96,512]{4,3,2,1,0:T(8,128)S(1)} %substeps.1) | data formatting | bytes 4718592

commit v5 on v4

--- a/solution.py
+++ b/solution.py
@@ -20,7 +20,7 @@
     return pltpu.roll(field, amount % field.shape[axis], axis)
 
 
-def sweep(load, emit, tiles, relax, outside):
+def sweep(load, emit, tiles, relax, zone_index):
     columns = None
     pending = [None] * SUBSTEPS
 
@@ -30,13 +30,13 @@
         turned = rotated(new_pressure, -1, 0)
         if above is not None:
             turned = jnp.where(row == TILE - 1, rotated(above, -1, 0), turned)
+        elif zone_index == tiles - 1:
+            turned = jnp.where(row == TILE - 1, 0.0, turned)
         new_x = along_x - (turned - new_pressure)
         fields = [new_pressure, new_x, new_y]
-        if relax is not None and index == 1:
+        if index == zone_index:
             weight, targets = relax
             fields = [f + weight * (b - f) for f, b in zip(fields, targets)]
-        if outside and index == 0:
-            fields[1] = jnp.zeros_like(new_x)
         push(stage + 1, index, stiff, fields)
 
     def push(stage, index, stiff, fields):
@@ -49,6 +49,8 @@
         before = pending[stage]
         if before is not None:
             turned = jnp.where(row == 0, rotated(before[3], 1, 0), turned)
+        elif zone_index == 0:
+            turned = jnp.where(row == 0, 0.0, turned)
         flow = (along_x - turned) + (along_y - rotated(along_y, 1, 1))
         new_pressure = pressure - stiff * flow
         new_y = along_y - (rotated(new_pressure, -1, 1) - new_pressure)
@@ -119,16 +121,6 @@
         loads(level).start()
     rows_load.start()
 
-    @pl.when(bottom)
-    def _():
-        fields[:, :, :TILE, :] = jnp.zeros((3, levels, TILE, columns), jnp.float32)
-        stiff[:, :TILE, :] = jnp.zeros((levels, TILE, columns), jnp.float32)
-
-    @pl.when(top)
-    def _():
-        fields[:, :, TILE + rows:, :] = jnp.zeros((3, levels, TILE, columns), jnp.float32)
-        stiff[:, TILE + rows:, :] = jnp.zeros((levels, TILE, columns), jnp.float32)
-
     half = parts // 2
     own_load.wait()
     for part in range(half):
@@ -210,7 +202,7 @@
             for f in range(3):
                 out[0, f, level, pl.ds(TILE + TILE * index, TILE), :] = values[f]
 
-        sweep(load, emit, rows // TILE - 2, None, False)
+        sweep(load, emit, rows // TILE - 2, None, None)
         return carry
 
     split = levels // 4
@@ -251,7 +243,7 @@
 
     low_weight = weights(row, bottom)
     high_weight = weights(ZONE - 1 - row, top)
-    def strip(level, base, weight, outside, emit):
+    def strip(level, base, weight, zone_index, emit):
         def load(index):
             at_rows = pl.ds(base + TILE * index, TILE)
             return stiff[level, at_rows, :], [fields[f, level, at_rows, :] for f in range(3)]
@@ -260,17 +252,20 @@
         if weight is not None:
             relax = (weight, [jnp.concatenate([zone[g, level, f] for g in range(groups)], axis=-1)
                               for f in range(3)])
-        sweep(load, emit, 3, relax, outside)
+        sweep(load, emit, 3 if weight is None else 2, relax, zone_index)
 
     def low_strip(level, weight):
+        skip = 0 if weight is None else 1
+
         def emit(index, values):
+            index = index + skip
             for f in range(3):
                 if index == 1:
                     out[0, f, level, pl.ds(0, TILE), :] = values[f]
                 if index == 2:
                     out[0, f, level, pl.ds(TILE, HALO), :] = values[f][:HALO]
 
-        strip(level, 0, weight, weight is not None, emit)
+        strip(level, TILE * skip, weight, None if weight is None else 0, emit)
 
     def high_strip(level, weight):
         def emit(index, values):
@@ -280,7 +275,7 @@
                 if index == 1:
                     out[0, f, level, pl.ds(rows - TILE, TILE), :] = values[f]
 
-        strip(level, rows - TILE, weight, False, emit)
+        strip(level, rows - TILE, weight, None if weight is None else 1, emit)
 
     def zone_arrival():
         for j in range(1, groups):

time: 16.5 us -> 16.5 us (level)
  no operation moved by 1% of the time
where the time goes in v5:
time: 16.5 us; the launch traced here: 16.4 us
  Pallas kernels  14.3 us (87%)
  local copies, waits for them, and re-layouts  1.41 us (9%)
  between operations  0.66 us (4%)
    pallas_call x1, Pallas kernels, body(): pl.pallas_call(functools.partial(kernel, members, tiles), out_shape=jax.S...  14.3 us
    unnamed x1, local copies, waits for them, and re-layouts  1.41 us

profile of v5, /device:TPU:0, one launch (start us, length us, event | category | flops | bytes accessed | tf_op | source)
XLA Modules:
  0.0 16.4 jit_solution(2144440624698636783)
XLA Ops:
  0.7 14.3 %substeps.1 = f32[1,3,4,96,512]{4,3,2,1,0:T(8,128)S(1)} custom-call(s32[1]{0:T(128)S(6)} %copy.7.zone_depth, s32[16]{0:T(128)} %zone_rows_hbm.1, f32[1,3,4,96,512]{4,3,2,1,0:T(8,128)} %state.1, f32[4,96,512]{2,1,0:T(8,128)} %stiffness.1, f32[12,4,64]{2,1,0:T(4,128)} %bitcast.1), custom_call_target="tpu_custom_call" | custom-call | tf_op jit(solution)/shard_map/substeps/pallas_call | solution.py:362
  15.0 1.4 %copy.8 = f32[1,3,4,96,512]{4,3,2,1,0:T(8,128)} copy(f32[1,3,4,96,512]{4,3,2,1,0:T(8,128)S(1)} %substeps.1) | data formatting | bytes 4718592
